TPU v7x, 256 devices: a whole 4x4x8 slice. The times are simulated.
256 devices in a mesh: grp: 2 (over y_lo), gy: 8 (over x, core), gz: 16 (over y_hi, z).
Axes of the slice: x: 4, y: 4 (y_hi: 2, y_lo: 2; y = y_hi * 2 + y_lo), z: 8, core: 2. Of those that a mesh axis runs over, the one named last changes fastest.
Arguments:
- offsets: float32 [2, 16, 128, 3, 128], P('grp', 'gy', 'gz'), may hold values from 0 to 1
- nbr_list: int32 [2, 16, 128, 9], P('grp', 'gy', 'gz'), may hold values from 0 to 8, as said below
- nbr_count: int32 [2, 16, 128], P('grp', 'gy', 'gz'), may hold values from 1 to 9, as said below
- source: float32 [2, 16, 128, 128], P('grp', 'gy', 'gz'), may hold values from -180 to 180
- start_p: float32 [2, 16, 128, 128], P('grp', 'gy', 'gz'), may hold values from -6 to 6
- guard_coef: float32 [2, 8, 16, 16, 128], P('grp', 'gy', 'gz'), may hold values from 10 to 100
- send_block: int32 [2, 8, 16, 8], P('grp', 'gy', 'gz'), may hold values from 0 to 15
- send_tile: int32 [2, 8, 16, 8], P('grp', 'gy', 'gz'), may hold values from 0 to 127
- send_guard: int32 [2, 8, 16, 8], P('grp', 'gy', 'gz'), may hold values from 0 to 15
- send_count: int32 [2, 8, 16], P('grp', 'gy', 'gz'), may hold values from 1 to 8, as said below
- interp: float32 [2, 8, 16, 8, 128, 128], P('grp', 'gy', 'gz'), may hold values from -0.5 to 0.5
Outputs:
- pressure: float32 [2, 16, 128, 128], P('grp', 'gy', 'gz')
Inputs may be any that keep to these rules, and one draw needn't show every extreme that they name: `nbr_list`: the entries of one block's list are distinct slot codes. `nbr_count`: every draw has a block with all 9 slots live in each tile. `send_count`: every draw has, in some tile of each group, all 8 outgoing interpolations live.
All inputs are finite; a program needn't handle non-finite values.
Results may differ from a plain program's by a relative error of at most 0.0001.
Values sent between devices are 32-bit elements; how exact they have to be, the bound alone decides.
A program may use at most 64 MiB of HBM per device.

v0:
```python
import jax
import jax.numpy as jnp
from jax import lax
from jax.sharding import PartitionSpec as P

PB = 128
SLOTS = 9
ITERS = 3


KERNEL_WIDTH = 0.5


def with_halo(cells, sides, width):
    for axis, dim in sides:
        count = lax.axis_size(axis)
        head = lax.slice_in_dim(cells, 0, width, axis=dim)
        tail = lax.slice_in_dim(cells, cells.shape[dim] - width, cells.shape[dim], axis=dim)
        cells = jnp.concatenate(
            [
                lax.ppermute(tail, axis, [(i, (i + 1) % count) for i in range(count)]),
                cells,
                lax.ppermute(head, axis, [((i + 1) % count, i) for i in range(count)]),
            ],
            axis=dim,
        )
    return cells


def partner(value, axis, stride):
    return lax.ppermute(value, axis, [(i, i ^ 1 << stride) for i in range(lax.axis_size(axis))])


def rim_pressure(pressure):
    return with_halo(pressure, (("gy", 1), ("gz", 2)), 1)


def local(
    offsets,
    nbr_list,
    nbr_count,
    source,
    start_p,
    guard_coef,
    send_block,
    send_tile,
    send_guard,
    send_count,
    interp,
):
    rows_y = offsets.shape[1]
    cols_z = offsets.shape[2]
    blocks = rows_y * cols_z
    guards_in = guard_coef.shape[3]
    slots_out = send_block.shape[3]
    tiles_all = lax.axis_size(("gy", "gz"))
    rim_offsets = with_halo(offsets, (("gy", 1), ("gz", 2)), 1)
    live = jnp.arange(SLOTS, dtype=jnp.int32)[None, None, None, :] < nbr_count[..., None]
    coef_full = jnp.concatenate(
        [guard_coef[0, 0, 0], jnp.zeros((blocks - guards_in, PB), jnp.float32)], axis=0
    ).reshape(1, rows_y, cols_z, PB)
    slot_live = (jnp.arange(slots_out, dtype=jnp.int32) < send_count[0, 0, 0]).astype(jnp.float32)
    dest_code = send_tile[0, 0, 0] * guards_in + send_guard[0, 0, 0]
    weight_tables = []
    active_list = []
    denom = jnp.zeros_like(start_p)
    for step_y in (-1, 0, 1):
        for step_z in (-1, 0, 1):
            slot_code = 3 * (step_y + 1) + (step_z + 1)
            near_off = rim_offsets[
                :, 1 + step_y : 1 + step_y + rows_y, 1 + step_z : 1 + step_z + cols_z
            ]
            shift_vec = jnp.array([0.0, float(step_y), float(step_z)], jnp.float32)
            diff = offsets[..., :, :, None] - (near_off[..., :, None, :] + shift_vec[:, None, None])
            weight = jnp.exp(-jnp.sum(diff * diff, axis=-3) / KERNEL_WIDTH)
            active = jnp.sum(((nbr_list == slot_code) & live).astype(jnp.float32), axis=-1)[
                ..., None
            ]
            denom = denom + active * jnp.sum(weight, axis=-1)
            active_list.append(active)
            weight_tables.append(weight)
    pressure = start_p
    for sweep_no in range(ITERS):
        rim_p = rim_pressure(pressure)
        numer = jnp.zeros_like(pressure)
        position = 0
        for step_y in (-1, 0, 1):
            for step_z in (-1, 0, 1):
                near_p = rim_p[
                    :, 1 + step_y : 1 + step_y + rows_y, 1 + step_z : 1 + step_z + cols_z
                ]
                weighted = jnp.einsum(
                    "gyzij,gyzj->gyzi",
                    weight_tables[position],
                    near_p,
                    precision=lax.Precision.HIGHEST,
                )
                numer = numer + active_list[position] * weighted
                position += 1
        tile_blocks = pressure.reshape(blocks, PB)
        chosen = tile_blocks[send_block[0, 0, 0]]
        values = jnp.einsum("sij,sj->si", interp[0, 0, 0], chosen, precision=lax.Precision.HIGHEST)
        values = values * slot_live[:, None]
        onehot = (
            dest_code[:, None] == jnp.arange(tiles_all * guards_in, dtype=jnp.int32)[None, :]
        ).astype(jnp.float32)
        buckets = jnp.dot(onehot.T, values, precision=lax.Precision.HIGHEST).reshape(
            tiles_all, guards_in, PB
        )
        mine = lax.psum_scatter(buckets, ("gy", "gz"), scatter_dimension=0, tiled=True)
        guard_p = partner(mine, "grp", 0)
        guard_full = jnp.concatenate(
            [guard_p[0], jnp.zeros((blocks - guards_in, PB), jnp.float32)], axis=0
        ).reshape(1, rows_y, cols_z, PB)
        pressure = (numer + coef_full * guard_full - source) / (denom + coef_full + 1.0)
    return pressure


def solution(mesh):
    placed = (
        P("grp", "gy", "gz", None, None),
        P("grp", "gy", "gz", None),
        P("grp", "gy", "gz"),
        P("grp", "gy", "gz", None),
        P("grp", "gy", "gz", None),
        P("grp", "gy", "gz", None, None),
        P("grp", "gy", "gz", None),
        P("grp", "gy", "gz", None),
        P("grp", "gy", "gz", None),
        P("grp", "gy", "gz"),
        P("grp", "gy", "gz", None, None, None),
    )
    return jax.shard_map(
        local, mesh=mesh, in_specs=placed, out_specs=P("grp", "gy", "gz", None), check_vma=False
    )
```

profile of v0, /device:TPU:1, one launch (start us, length us, event | category | flops | bytes accessed | tf_op | source)
XLA Modules:
  0.0 1979.2 jit_solution(8705730644162696603)
XLA Ops:
  6.5 0.7 fusion.90
  7.9 0.7 add_bitcast_fusion
  8.6 1.2 gather_fusion
  9.9 0.9 fusion.4
  10.8 2.1 fusion.44
  13.1 2.6 collective-permute-start.3
  15.7 0.7 collective-permute-start.4
  16.3 1.1 collective-permute-start
  17.4 1.9 collective-permute-start.1
  19.3 1.1 collective-permute-start.5
  20.4 6.7 collective-permute-start.7
  27.3 0.7 collective-permute-done.5
  28.1 5.2 collective-permute-start.6
  33.4 0.7 collective-permute-done.6
  34.1 5.5 collective-permute-done.2
  39.9 5.2 multiply_reduce_fusion.8
  45.1 1.8 fusion.37
  46.9 0.6 fusion.32
  47.5 0.6 fusion.24
  48.2 0.6 fusion.16
  49.4 1.8 fusion.33
  51.2 1.8 fusion.29
  53.0 1.8 fusion.25
  54.8 1.8 fusion.21
  56.5 1.8 fusion.17
  58.3 1.8 fusion.13
  60.1 1.9 fusion.9
  62.0 1.8 fusion.41
  63.8 580.9 %reduce-scatter.4.cloned.1.call-done = f32[1,16,128]{2,1,0:T(8,128)} async-done(((f32[128,16,128]{2,1,0:T(8,128)}), f32[1,16,128]{2,1,0:T(8,128)}) %reduce-scatter.4.cloned.1.call-update) | async-done | bytes 8208 | tf_op jit(solution)/shard_map/reduce_scatter | solution.py:110
  645.0 1.6 fusion.40
  646.6 1.2 collective-permute-done.8
  648.5 0.9 fusion.2
  649.4 35.5 %collective-permute-start.10 = (f32[1,1,8,128]{3,2,1,0:T(8,128)S(1)}, f32[1,1,8,128]{3,2,1,0:T(8,128)S(1)}, u32[]{:S(2)}, u32[]{:S(2)}) collective-permute-start(f32[1,1,8,128]{3,2,1,0:T(8,128)S(1)} %get-tuple-element.74), channel_id=1, source_target_pairs={{16,0},{32,16},{48,32},{64,48},{80,64},{96,80},{112,96},{0,112},{1... | collective-permute-start | bytes 12296 | tf_op jit(solution)/shard_map/ppermute | solution.py:23
  684.9 2.1 fusion.43
  687.2 3.1 fusion.23
  690.3 1.6 collective-permute-start.11
  692.0 4.6 collective-permute-done.11
  696.6 1.8 fusion.39
  698.4 1.8 fusion.35
  700.2 1.8 fusion.31
  702.0 1.8 fusion.27
  703.7 1.8 fusion.19
  705.5 1.8 fusion.15
  707.3 1.8 fusion.11
  709.1 597.4 %reduce-scatter.6.cloned.1.call-done = f32[1,16,128]{2,1,0:T(8,128)} async-done(((f32[128,16,128]{2,1,0:T(8,128)}), f32[1,16,128]{2,1,0:T(8,128)}) %reduce-scatter.6.cloned.1.call-update) | async-done | bytes 8208 | tf_op jit(solution)/shard_map/reduce_scatter | solution.py:110
  1307.1 1.8 fusion.7
  1308.8 1.0 collective-permute-done.13
  1310.5 0.9 fusion
  1311.4 35.3 %collective-permute-start.15 = (f32[1,1,8,128]{3,2,1,0:T(8,128)S(1)}, f32[1,1,8,128]{3,2,1,0:T(8,128)S(1)}, u32[]{:S(2)}, u32[]{:S(2)}) collective-permute-start(f32[1,1,8,128]{3,2,1,0:T(8,128)S(1)} %get-tuple-element.72), channel_id=1, source_target_pairs={{16,0},{32,16},{48,32},{64,48},{80,64},{96,80},{112,96},{0,112},{1... | collective-permute-start | bytes 12296 | tf_op jit(solution)/shard_map/ppermute | solution.py:23
  1346.8 2.1 fusion.42
  1349.0 3.1 fusion.22
  1352.1 1.7 collective-permute-start.16
  1353.8 4.6 collective-permute-done.16
  1358.5 1.8 fusion.38
  1360.2 1.8 fusion.34
  1362.0 1.8 fusion.30
  1363.8 1.8 fusion.26
  1365.6 1.8 fusion.18
  1367.4 1.8 fusion.14
  1369.1 1.8 fusion.10
  1370.9 597.4 %reduce-scatter.8.cloned.1.call-done = f32[1,16,128]{2,1,0:T(8,128)} async-done(((f32[128,16,128]{2,1,0:T(8,128)}), f32[1,16,128]{2,1,0:T(8,128)}) %reduce-scatter.8.cloned.1.call-update) | async-done | bytes 8208 | tf_op jit(solution)/shard_map/reduce_scatter | solution.py:110
  1968.5 1.8 fusion.6
  1970.3 1.1 collective-permute-done.18
  1971.4 0.7 fusion.60
  (131 shorter events, 4.0 us)
Async XLA Ops:
  6.5 3.3 copy-start
  6.5 638.2 %reduce-scatter.4.cloned.1.call-start = ((), (), s32[]{:S(2)}) async-start(), calls=%async_computation.3 | async-start | bytes 1056768 | tf_op jit(solution)/shard_map/reduce_scatter | solution.py:110
  10.8 2.2 copy-start.20
  10.8 5.5 copy-start.21
  10.8 16.3 copy-start.24
  10.8 16.3 copy-start.25
  10.8 22.5 %copy-start.32 = (f32[3]{0:T(128)S(1)}, f32[3]{0:T(128)}, u32[]{:S(2)}) copy-start(f32[3]{0:T(128)} %constant.61.clone) | copy-start | bytes 40
  10.8 22.5 %copy-start.33 = (f32[3]{0:T(128)S(1)}, f32[3]{0:T(128)}, u32[]{:S(2)}) copy-start(f32[3]{0:T(128)} %constant.55.clone) | copy-start | bytes 40
  12.9 26.7 %copy-start.26 = (f32[3]{0:T(128)S(1)}, f32[3]{0:T(128)}, u32[]{:S(2)}) copy-start(f32[3]{0:T(128)} %constant.62.clone) | copy-start | bytes 40
  12.9 26.7 %copy-start.27 = (f32[3]{0:T(128)S(1)}, f32[3]{0:T(128)}, u32[]{:S(2)}) copy-start(f32[3]{0:T(128)} %constant.59.clone) | copy-start | bytes 40
  12.9 26.7 %copy-start.28 = (f32[3]{0:T(128)S(1)}, f32[3]{0:T(128)}, u32[]{:S(2)}) copy-start(f32[3]{0:T(128)} %constant.56.clone) | copy-start | bytes 40
  12.9 26.7 %copy-start.29 = (f32[3]{0:T(128)S(1)}, f32[3]{0:T(128)}, u32[]{:S(2)}) copy-start(f32[3]{0:T(128)} %constant.54.clone) | copy-start | bytes 40
  12.9 26.7 %copy-start.30 = (f32[3]{0:T(128)S(1)}, f32[3]{0:T(128)}, u32[]{:S(2)}) copy-start(f32[3]{0:T(128)} %constant.57.clone) | copy-start | bytes 40
  12.9 26.7 %copy-start.31 = (f32[3]{0:T(128)S(1)}, f32[3]{0:T(128)}, u32[]{:S(2)}) copy-start(f32[3]{0:T(128)} %constant.60.clone) | copy-start | bytes 40
  13.0 1293.5 %reduce-scatter.6.cloned.1.call-start = ((), (), s32[]{:S(2)}) async-start(), calls=%async_computation.4 | async-start | bytes 1056768 | tf_op jit(solution)/shard_map/reduce_scatter | solution.py:110
  13.1 6.2 collective-permute-start.3
  15.7 3.6 collective-permute-start.4
  16.3 11.7 collective-permute-start
  17.4 10.6 collective-permute-start.1
  19.3 8.6 collective-permute-start.5
  20.4 7.5 collective-permute-start.7
  28.1 6.0 collective-permute-start.6
  33.3 6.3 collective-permute-start.2
  45.1 3.7 copy-start.13
  45.1 4.4 copy-start.10
  45.1 6.1 copy-start.7
  45.1 7.9 copy-start.19
  45.1 9.7 copy-start.4
  45.1 11.4 copy-start.1
  45.1 16.9 copy-start.16
  62.0 585.8 %copy-start.22 = (f32[1,2,8,128]{3,2,1,0:T(8,128)S(1)}, f32[1,2,8,128]{3,2,1,0:T(8,128)}, u32[]{:S(2)}) copy-start(f32[1,2,8,128]{3,2,1,0:T(8,128)} %param.23) | copy-start | bytes 24580
  62.0 585.8 %copy-start.23 = (f32[1,1,1,16,128]{4,3,2,1,0:T(8,128)S(1)}, f32[1,1,1,16,128]{4,3,2,1,0:T(8,128)}, u32[]{:S(2)}) copy-start(f32[1,1,1,16,128]{4,3,2,1,0:T(8,128)} %param.25) | copy-start | bytes 24580
  644.7 3.1 collective-permute-start.8
  649.4 37.7 %collective-permute-start.10 = (f32[1,1,8,128]{3,2,1,0:T(8,128)S(1)}, f32[1,1,8,128]{3,2,1,0:T(8,128)S(1)}, u32[]{:S(2)}, u32[]{:S(2)}) collective-permute-start(f32[1,1,8,128]{3,2,1,0:T(8,128)S(1)} %get-tuple-element.74), channel_id=1, source_target_pairs={{16,0},{32,16},{48,32},{64,48},{80,64},{96,80},{112,96},{0,112},{1... | collective-permute-start | bytes 12296 | tf_op jit(solution)/shard_map/ppermute | solution.py:23
  684.9 2.2 collective-permute-start.9
  687.0 1281.3 %reduce-scatter.8.cloned.1.call-start = ((), (), s32[]{:S(2)}) async-start(), calls=%async_computation.5 | async-start | bytes 1056768 | tf_op jit(solution)/shard_map/reduce_scatter | solution.py:110
  687.1 9.5 copy-start.17
  687.1 4.8 collective-permute-start.12
  687.2 11.2 copy-start.14
  690.3 6.3 collective-permute-start.11
  696.6 3.6 copy-start.11
  698.4 3.6 copy-start.8
  700.2 3.6 copy-start.5
  702.0 3.6 copy-start.2
  1306.5 3.3 collective-permute-start.13
  1311.4 37.4 %collective-permute-start.15 = (f32[1,1,8,128]{3,2,1,0:T(8,128)S(1)}, f32[1,1,8,128]{3,2,1,0:T(8,128)S(1)}, u32[]{:S(2)}, u32[]{:S(2)}) collective-permute-start(f32[1,1,8,128]{3,2,1,0:T(8,128)S(1)} %get-tuple-element.72), channel_id=1, source_target_pairs={{16,0},{32,16},{48,32},{64,48},{80,64},{96,80},{112,96},{0,112},{1... | collective-permute-start | bytes 12296 | tf_op jit(solution)/shard_map/ppermute | solution.py:23
  1346.8 2.1 collective-permute-start.14
  1348.9 9.6 copy-start.18
  1348.9 4.9 collective-permute-start.17
  1349.0 11.3 copy-start.15
  1352.1 6.4 collective-permute-start.16
  1358.5 3.6 copy-start.12
  1360.2 3.6 copy-start.9
  1362.0 3.6 copy-start.6
  1363.8 3.6 copy-start.3
  1968.3 3.1 collective-permute-start.18
Sparse Core Ops, SparseCore 0:
  13.1 631.5 reduce-scatter.3
  687.2 619.3 reduce-scatter.5
  1349.0 619.2 reduce-scatter.7
where the time goes:
time: 2020 us; the launch traced here: 1980 us
  waiting for transfers between devices  1800 us (89%)
  starting transfers between devices  94.7 us (5%)
  matrix products  59.6 us (3%)
    reduce_scatter x3, waiting for transfers between devices, local(): lax.psum_scatter(buckets, ('gy', 'gz'), scatter_dimension=0, tiled=True)  1780 us
    ppermute x8, starting transfers between devices, with_halo(): lax.ppermute(head, axis, [((i + 1) % count, i) for i in range(count)])  85.4 us
    dot_general x27, matrix products, local(): jnp.einsum('gyzij,gyzj->gyzi', weight_tables[position], near_p, precision...  50.6 us
  transfers between devices with their start and end apart: 22, of which 11 were waited for; matrix products, arithmetic and copies ran while one was open for 3% of the time, Pallas kernels for 0%

commit v1 on v0

v1 whole, which is shorter than its diff:
```python
import functools
import math

import jax
import jax.numpy as jnp
from jax import lax
from jax.experimental import pallas as pl
from jax.experimental.pallas import tpu as pltpu
from jax.sharding import PartitionSpec as P

PB = 128
SLOTS = 9
ITERS = 3
KERNEL_WIDTH = 0.5
MESH = pl.DeviceIdType.MESH
KAPPA = math.sqrt(1.0 / (KERNEL_WIDTH * math.log(2.0)))
OFF = -1.0e4


def kernel(
    n_gy,
    n_gz,
    off_ref,
    list_ref,
    cnt_ref,
    src_ref,
    p_ref,
    gc_ref,
    sb_ref,
    st_ref,
    sg_ref,
    sc_ref,
    interp_ref,
    out_ref,
    ext0,
    own8,
    pext,
    pden,
    wts,
    mask,
    first,
    later,
    got_first,
    got,
    buckets,
    got_buckets,
    onehot,
    num,
    den,
    h_send,
    h_recv,
    g_send,
    g_recv,
    r_send,
    r_recv,
):
    g = lax.axis_index("grp")
    y = lax.axis_index("gy")
    z = lax.axis_index("gz")
    rows_y, cols_z = off_ref.shape[1], off_ref.shape[2]
    guards = gc_ref.shape[3]
    slots_out = sb_ref.shape[3]

    def at(gg, dy, dz):
        return (gg, lax.rem(y + dy + n_gy, n_gy), lax.rem(z + dz + n_gz, n_gz))

    partners = {(1, 0, o) for o in range(n_gz)}
    partners |= {(0, o, 0) for o in range(1, n_gy)}
    partners |= {
        (0, a % n_gy, b % n_gz) for a in (-1, 0, 1) for b in (-1, 0, 1) if (a, b) != (0, 0)
    }
    partners = sorted(partners)

    barrier = pltpu.get_barrier_semaphore()
    for flip, dy, dz in partners:
        pl.semaphore_signal(
            barrier,
            inc=1,
            device_id=at(1 - g if flip else g, dy, dz),
            device_id_type=MESH,
        )

    sides = []
    for dy in (-1, 0, 1):
        for dz in (-1, 0, 1):
            if (dy, dz) == (0, 0):
                continue
            ys = {-1: (1, 1), 0: (1, rows_y), 1: (rows_y, 1)}[dy]
            zs = {-1: (1, 1), 0: (1, cols_z), 1: (cols_z, 1)}[dz]
            yd = {-1: rows_y + 1, 0: 1, 1: 0}[dy]
            zd = {-1: cols_z + 1, 0: 1, 1: 0}[dz]
            sides.append((dy, dz, ys, zs, yd, zd))

    def send_halo(buf, sweep):
        for dy, dz, ys, zs, yd, zd in sides:
            pltpu.make_async_remote_copy(
                src_ref=buf.at[pl.ds(ys[0], ys[1]), pl.ds(zs[0], zs[1])],
                dst_ref=buf.at[pl.ds(yd, ys[1]), pl.ds(zd, zs[1])],
                send_sem=h_send.at[sweep],
                recv_sem=h_recv.at[sweep],
                device_id=at(g, dy, dz),
                device_id_type=MESH,
            ).start()

    rim = 2 * cols_z + 2 * rows_y + 4

    def rim_wait(buf, sem):
        part = buf.at[pl.ds(0, rim // cols_z), pl.ds(0, cols_z)]
        pltpu.make_async_copy(part, part, sem).wait()

    def send_values(src, dst, sweep):
        order = sorted(range(n_gz), key=lambda o: -min(o, n_gz - o))
        for o in order:
            pltpu.make_async_remote_copy(
                src_ref=src,
                dst_ref=dst.at[o],
                send_sem=g_send.at[sweep],
                recv_sem=g_recv.at[sweep],
                device_id=at(1 - g, 0, o),
                device_id_type=MESH,
            ).start()

    def send_buckets(sweep):
        order = sorted(range(1, n_gy), key=lambda o: -min(o, n_gy - o))
        for o in order:
            to = lax.rem(y + o, n_gy)
            pltpu.make_async_remote_copy(
                src_ref=buckets.at[sweep, to],
                dst_ref=got_buckets.at[sweep, o - 1],
                send_sem=r_send.at[sweep],
                recv_sem=r_recv.at[sweep],
                device_id=at(g, o, 0),
                device_id_type=MESH,
            ).start()

    def whole_wait(ref, sem):
        pltpu.make_async_copy(ref, ref, sem).wait()

    row_id = lax.broadcasted_iota(jnp.int32, (PB, PB), 0)
    lane_id = lax.broadcasted_iota(jnp.int32, (PB, PB), 1)
    eye = row_id == lane_id

    def row_sums(acc):
        total = jnp.sum(acc, axis=1, keepdims=True)
        return jnp.sum(jnp.where(eye, total, 0.0), axis=0, keepdims=True)

    def interpolate(dst):
        for s in range(slots_out):
            press = pden[pl.ds(sb_ref[0, 0, 0, s], 1), :]
            dst[pl.ds(s, 1), :] = row_sums(interp_ref[0, 0, 0, s] * press)

    for a in range(rows_y):
        for b in range(cols_z):
            scaled = (off_ref[0, a, b] - 0.5) * (2.0 * KAPPA)
            ext0[1 + a, 1 + b, pl.ds(0, 3), :] = scaled
            ext0[1 + a, 1 + b, pl.ds(3, 1), :] = p_ref[0, a, pl.ds(b, 1), :]
            own8[a, b, pl.ds(0, 3), :] = scaled * 0.5
        pden[pl.ds(a * cols_z, cols_z), :] = p_ref[0, a]

    interpolate(first)
    codes = jnp.full((slots_out, PB), -1, jnp.int32)
    slot_row = lax.broadcasted_iota(jnp.int32, (slots_out, PB), 0)
    for s in range(slots_out):
        codes = jnp.where(slot_row == s, st_ref[0, 0, 0, s] * guards + sg_ref[0, 0, 0, s], codes)
    codes = jnp.where(slot_row < sc_ref[0, 0, 0], codes, -1)
    first[pl.ds(slots_out, slots_out), :] = codes.astype(jnp.float32)

    pl.semaphore_wait(barrier, len(partners))
    send_values(first, got_first, 0)
    send_halo(ext0, 0)

    for a in range(rows_y):
        lanes = lax.broadcasted_iota(jnp.int32, (cols_z, cols_z), 1)
        subs = lax.broadcasted_iota(jnp.int32, (cols_z, cols_z), 0)
        counts = jnp.sum(
            jnp.where(lanes == subs, cnt_ref[0, pl.ds(a, 1), :], 0).astype(jnp.float32),
            axis=1,
            keepdims=True,
        )
        places = lax.broadcasted_iota(jnp.int32, (cols_z, SLOTS), 1).astype(jnp.float32)
        for c in range(SLOTS):
            hit = (list_ref[0, a] == c) & (places < counts)
            active = jnp.sum(jnp.where(hit, 1.0, 0.0), axis=1, keepdims=True)
            mask[c, a] = jnp.broadcast_to((1.0 - active) * OFF, (cols_z, PB))

    def own_columns(a, b):
        cols = jnp.transpose(own8[a, b])
        cx = jnp.broadcast_to(cols[:, 0:1], (PB, PB))
        cy = jnp.broadcast_to(cols[:, 1:2], (PB, PB))
        cz = jnp.broadcast_to(cols[:, 2:3], (PB, PB))
        return cx, cy, cz, -(cx * cx + cy * cy + cz * cz)

    def make_weights(a, b, pairs):
        cx, cy, cz, cn = own_columns(a, b)
        for dy, dz in pairs:
            c = 3 * (dy + 1) + (dz + 1)
            near = ext0[1 + a + dy, 1 + b + dz]
            rx = near[0:1]
            ry = near[1:2] + 2.0 * KAPPA * dy
            rz = near[2:3] + 2.0 * KAPPA * dz
            rn = mask[c, a, pl.ds(b, 1), :] - 0.25 * (rx * rx + ry * ry + rz * rz)
            wts[a, b, c] = jnp.exp2((cn + rn) + (cx * rx + cy * ry) + cz * rz)

    all_dz = (-1, 0, 1)

    def inner(b, carry):
        for a in range(rows_y):
            dys = [dy for dy in (-1, 0, 1) if 0 <= a + dy < rows_y]
            make_weights(a, b, [(dy, dz) for dy in dys for dz in all_dz])
        return carry

    def outer(b, carry):
        for a in range(rows_y):
            dys = [dy for dy in (-1, 0, 1) if not 0 <= a + dy < rows_y]
            make_weights(a, b, [(dy, dz) for dy in dys for dz in all_dz])
        return carry

    def ends(t, carry):
        for a in range(rows_y):
            make_weights(
                a, t * (cols_z - 1), [(dy, dz) for dy in (-1, 0, 1) for dz in all_dz]
            )
        return carry

    def deliver(values, sweep):
        hi = values.astype(jnp.bfloat16)
        rest = values - hi.astype(jnp.float32)
        mid = rest.astype(jnp.bfloat16)
        low = (rest - mid.astype(jnp.float32)).astype(jnp.bfloat16)
        sel = onehot[...]
        total = jnp.dot(sel, hi, preferred_element_type=jnp.float32)
        total += jnp.dot(sel, mid, preferred_element_type=jnp.float32)
        total += jnp.dot(sel, low, preferred_element_type=jnp.float32)
        buckets[sweep] = total.reshape(n_gy, guards, PB)
        send_buckets(sweep)

    def sums(near_row, with_den):
        def body(b, carry):
            rows = [[near_row(e, b + k) for k in range(3)] for e in range(rows_y + 2)]
            for a in range(rows_y):
                acc = None
                tot = None
                for c in range(SLOTS):
                    w = wts[a, b, c]
                    part = w * rows[a + c // 3][c % 3]
                    acc = part if acc is None else acc + part
                    if with_den:
                        tot = w if tot is None else tot + w
                num[a, pl.ds(b, 1), :] = row_sums(acc)
                if with_den:
                    den[a, pl.ds(b, 1), :] = row_sums(tot)
            return carry

        lax.fori_loop(0, cols_z, body, 0)

    lax.fori_loop(1, cols_z - 1, inner, 0)

    whole_wait(got_first, g_recv.at[0])
    entries = n_gz * slots_out
    dest = n_gy * guards
    code_rows = got_first[:, pl.ds(slots_out, slots_out), :].reshape(entries, PB)[:, :dest]
    lane = lax.broadcasted_iota(jnp.int32, (entries, dest), 1)
    wanted = (lane // guards * n_gz + z) * guards + lax.rem(lane, guards)
    hits = jnp.where(code_rows == wanted.astype(jnp.float32), 1.0, 0.0)
    onehot[...] = jnp.transpose(hits).astype(jnp.bfloat16)
    deliver(got_first[:, pl.ds(0, slots_out), :].reshape(entries, PB), 0)

    rim_wait(ext0, h_recv.at[0])
    lax.fori_loop(1, cols_z - 1, outer, 0)
    lax.fori_loop(0, 2, ends, 0)

    sums(lambda e, k: ext0[e, k, pl.ds(3, 1), :], True)
    coef = gc_ref[0, 0, 0].reshape(rows_y, cols_z, PB)
    scale = 1.0 / (den[...] + coef + 1.0)

    for sweep in range(ITERS):
        base = num[...] - src_ref[0]
        whole_wait(got_buckets.at[sweep], r_recv.at[sweep])
        mine = buckets[sweep, y]
        for o in range(n_gy - 1):
            mine = mine + got_buckets[sweep, o]
        new = (base + coef * mine.reshape(rows_y, cols_z, PB)) * scale
        if sweep == ITERS - 1:
            out_ref[0] = new
            break
        pden[...] = new.reshape(rows_y * cols_z, PB)
        interpolate(later.at[sweep])
        send_values(later.at[sweep], got.at[sweep], sweep + 1)
        press = pext.at[sweep]
        for a in range(rows_y):
            for b in range(cols_z):
                press[1 + a, 1 + b] = new[a, b : b + 1]
        send_halo(press, sweep + 1)
        rim_wait(press, h_recv.at[sweep + 1])
        whole_wait(got.at[sweep], g_recv.at[sweep + 1])
        deliver(got[sweep].reshape(entries, PB), sweep + 1)
        sums(lambda e, k: press[e, k], False)

    rim_wait(ext0, h_send.at[0])
    whole_wait(got_first, g_send.at[0])
    for sweep in range(ITERS):
        whole_wait(got_buckets.at[sweep], r_send.at[sweep])
        if sweep:
            rim_wait(pext.at[sweep - 1], h_send.at[sweep])
            whole_wait(got.at[sweep - 1], g_send.at[sweep])


def local(n_gy, n_gz, *args):
    offsets, guard_coef, send_block = args[0], args[5], args[6]
    rows_y, cols_z = offsets.shape[1:3]
    guards = guard_coef.shape[3]
    slots_out = send_block.shape[3]
    f32 = jnp.float32
    vmem = pl.BlockSpec(memory_space=pltpu.VMEM)
    smem = pl.BlockSpec(memory_space=pltpu.SMEM)
    dma = pltpu.SemaphoreType.DMA((ITERS,))
    return pl.pallas_call(
        functools.partial(kernel, n_gy, n_gz),
        out_shape=jax.ShapeDtypeStruct((1, rows_y, cols_z, PB), f32),
        in_specs=[vmem] * 6 + [smem] * 4 + [vmem],
        out_specs=vmem,
        scratch_shapes=[
            pltpu.VMEM((rows_y + 2, cols_z + 2, 4, PB), f32),
            pltpu.VMEM((rows_y, cols_z, 8, PB), f32),
            pltpu.VMEM((ITERS - 1, rows_y + 2, cols_z + 2, 1, PB), f32),
            pltpu.VMEM((rows_y * cols_z, PB), f32),
            pltpu.VMEM((rows_y, cols_z, SLOTS, PB, PB), f32),
            pltpu.VMEM((SLOTS, rows_y, cols_z, PB), f32),
            pltpu.VMEM((2 * slots_out, PB), f32),
            pltpu.VMEM((ITERS - 1, slots_out, PB), f32),
            pltpu.VMEM((n_gz, 2 * slots_out, PB), f32),
            pltpu.VMEM((ITERS - 1, n_gz, slots_out, PB), f32),
            pltpu.VMEM((ITERS, n_gy, guards, PB), f32),
            pltpu.VMEM((ITERS, n_gy - 1, guards, PB), f32),
            pltpu.VMEM((n_gy * guards, n_gz * slots_out), jnp.bfloat16),
            pltpu.VMEM((rows_y, cols_z, PB), f32),
            pltpu.VMEM((rows_y, cols_z, PB), f32),
            dma,
            dma,
            dma,
            dma,
            dma,
            dma,
        ],
        compiler_params=pltpu.CompilerParams(
            collective_id=0, has_side_effects=True, vmem_limit_bytes=32 * 1024 * 1024
        ),
    )(*args)


def solution(mesh):
    placed = (
        P("grp", "gy", "gz", None, None),
        P("grp", "gy", "gz", None),
        P("grp", "gy", "gz"),
        P("grp", "gy", "gz", None),
        P("grp", "gy", "gz", None),
        P("grp", "gy", "gz", None, None),
        P("grp", "gy", "gz", None),
        P("grp", "gy", "gz", None),
        P("grp", "gy", "gz", None),
        P("grp", "gy", "gz"),
        P("grp", "gy", "gz", None, None, None),
    )
    return jax.shard_map(
        functools.partial(local, mesh.shape["gy"], mesh.shape["gz"]),
        mesh=mesh,
        in_specs=placed,
        out_specs=P("grp", "gy", "gz", None),
        check_vma=False,
    )
```

time: 2020 us -> 45.8 us (0.02); the launches traced: 1980 us -> 45.6 us
  waiting for transfers between devices: 1800 us -> 0 us
  starting transfers between devices: 94.7 us -> 0 us
  matrix products: 59.6 us -> 0 us
  Pallas kernels: 0 us -> 42.3 us
    reduce_scatter x3 -> x0, waiting for transfers between devices: 1780 us -> none  [local(): lax.psum_scatter(buckets, ('gy', 'gz'), scatter_dimension=0, tiled=True)]
    ppermute x19 -> x0, starting transfers between devices: 94.6 us -> none  [the longest x8 85.4 us: with_halo(): lax.ppermute(head, axis, [((i + 1) % count, i) for i in range(count)])]
    dot_general x33 -> x0, matrix products: 59.6 us -> none  [the longest x27 50.6 us: local(): jnp.einsum('gyzij,gyzj->gyzi', weight_tables[position], near_p, precision...]
    pallas_call x0 -> x1, Pallas kernels: none -> 42.3 us  [local(): pl.pallas_call(functools.partial(kernel, n_gy, n_gz), out_shape=jax.Shape...]
  transfers between devices with their start and end apart: 22 -> 0, of which waited for: 11 -> 0; matrix products, arithmetic and copies ran while one was open for 3% -> 0% of each run, Pallas kernels for 0% -> 0%
where the time goes in v1:
time: 45.8 us; the launch traced here: 45.6 us
  Pallas kernels  42.3 us (92%)
  local copies, waits for them, and re-layouts  2.46 us (5%)
  between operations  0.8 us (2%)
    pallas_call x1, Pallas kernels, local(): pl.pallas_call(functools.partial(kernel, n_gy, n_gz), out_shape=jax.Shape...  42.3 us
    unnamed x20, local copies, waits for them, and re-layouts  2.46 us

profile of v1, /device:TPU:1, one launch (start us, length us, event | category | flops | bytes accessed | tf_op | source)
XLA Modules:
  0.0 45.6 jit_solution(8934551830182930611)
XLA Ops:
  0.7 0.0 copy-start.1
  0.7 0.0 copy-start.2
  0.7 0.0 copy-start.3
  0.7 0.0 copy-start.4
  0.7 0.0 copy-start.5
  0.7 0.0 copy-start.6
  0.7 0.0 copy-start.7
  0.7 0.0 copy-start.8
  0.7 0.8 %copy.12.off_ref = f32[1,2,8,3,128]{4,3,2,1,0:T(4,128)S(1)} copy(f32[1,2,8,3,128]{4,2,3,1,0:T(8,128)} %param.11) | data formatting | bytes 49152 | tf_op args[0]
  1.5 0.0 copy-done.1
  1.5 0.0 copy-done.2
  1.5 0.0 copy-done.3
  1.6 0.0 copy-done.4
  1.6 0.0 copy-done.5
  1.6 0.0 copy-done.6
  1.6 0.0 copy-done.7
  1.6 0.0 copy-done.8
  1.6 0.0 copy-start
  1.6 1.0 %copy-done = f32[1,1,1,8,128,128]{5,4,3,2,1,0:T(8,128)S(1)} copy-done((f32[1,1,1,8,128,128]{5,4,3,2,1,0:T(8,128)S(1)}, f32[1,1,1,8,128,128]{5,4,3,2,1,0:T(8,128)}, u32[]{:S(2)}) %copy-start) | copy-done | bytes 524312
  2.7 42.3 %shard_map.109 = f32[1,2,8,128]{3,2,1,0:T(8,128)S(1)} custom-call(f32[1,2,8,3,128]{4,3,2,1,0:T(4,128)S(1)} %copy.12.off_ref, s32[1,2,8,9]{3,2,1,0:T(8,128)S(1)} %copy-done.1, s32[1,2,8]{2,1,0:T(2,128)S(1)} %copy-done.5, f32[1,2,8,128]{3,2,1,0:T(8,128)S(1)} %copy-done.2, f32[1,2,8,128]{3,2,1,0:T(8,128)S(1)} %copy-done.3, f32[1,1,1,16,128]{4,3,2,1,0:T(8,128)S(1)} %copy-done.4, ...), custom_call_target="tpu_custom_call" | custom-call | tf_op jit(solution)/shard_map/pallas_call | solution.py:317
  45.0 0.6 %copy.15 = f32[1,2,8,128]{3,2,1,0:T(8,128)} copy(f32[1,2,8,128]{3,2,1,0:T(8,128)S(1)} %shard_map.109) | data formatting | bytes 16384
Async XLA Ops:
  0.7 0.9 %copy-start.1 = (s32[1,2,8,9]{3,2,1,0:T(8,128)S(1)}, s32[1,2,8,9]{3,2,1,0:T(8,128)}, u32[]{:S(2)}) copy-start(s32[1,2,8,9]{3,2,1,0:T(8,128)} %list_ref.1) | copy-start | bytes 1732
  0.7 0.9 %copy-start.2 = (f32[1,2,8,128]{3,2,1,0:T(8,128)S(1)}, f32[1,2,8,128]{3,2,1,0:T(8,128)}, u32[]{:S(2)}) copy-start(f32[1,2,8,128]{3,2,1,0:T(8,128)} %src_ref.1) | copy-start | bytes 24580
  0.7 0.9 %copy-start.3 = (f32[1,2,8,128]{3,2,1,0:T(8,128)S(1)}, f32[1,2,8,128]{3,2,1,0:T(8,128)}, u32[]{:S(2)}) copy-start(f32[1,2,8,128]{3,2,1,0:T(8,128)} %p_ref.1) | copy-start | bytes 24580
  0.7 0.9 %copy-start.4 = (f32[1,1,1,16,128]{4,3,2,1,0:T(8,128)S(1)}, f32[1,1,1,16,128]{4,3,2,1,0:T(8,128)}, u32[]{:S(2)}) copy-start(f32[1,1,1,16,128]{4,3,2,1,0:T(8,128)} %gc_ref.1) | copy-start | bytes 24580
  0.7 0.9 %copy-start.5 = (s32[1,2,8]{2,1,0:T(2,128)S(1)}, s32[1,2,8]{2,1,0:T(2,128)}, u32[]{:S(2)}) copy-start(s32[1,2,8]{2,1,0:T(2,128)} %cnt_ref.1) | copy-start | bytes 196
  0.7 0.9 %copy-start.6 = (s32[1,1,1,8]{3,2,1,0:T(1,128)S(1)}, s32[1,1,1,8]{3,2,1,0:T(1,128)}, u32[]{:S(2)}) copy-start(s32[1,1,1,8]{3,2,1,0:T(1,128)} %sb_ref.1) | copy-start | bytes 100
  0.7 0.9 %copy-start.7 = (s32[1,1,1,8]{3,2,1,0:T(1,128)S(1)}, s32[1,1,1,8]{3,2,1,0:T(1,128)}, u32[]{:S(2)}) copy-start(s32[1,1,1,8]{3,2,1,0:T(1,128)} %st_ref.1) | copy-start | bytes 100
  0.7 0.9 %copy-start.8 = (s32[1,1,1,8]{3,2,1,0:T(1,128)S(1)}, s32[1,1,1,8]{3,2,1,0:T(1,128)}, u32[]{:S(2)}) copy-start(s32[1,1,1,8]{3,2,1,0:T(1,128)} %sg_ref.1) | copy-start | bytes 100
  1.6 1.0 %copy-start = (f32[1,1,1,8,128,128]{5,4,3,2,1,0:T(8,128)S(1)}, f32[1,1,1,8,128,128]{5,4,3,2,1,0:T(8,128)}, u32[]{:S(2)}) copy-start(f32[1,1,1,8,128,128]{5,4,3,2,1,0:T(8,128)} %interp_ref.1) | copy-start | bytes 1572868

commit v2 on v1

--- a/solution.py
+++ b/solution.py
@@ -20,18 +20,12 @@
 def kernel(
     n_gy,
     n_gz,
-    off_ref,
-    list_ref,
-    cnt_ref,
-    src_ref,
-    p_ref,
-    gc_ref,
-    sb_ref,
-    st_ref,
-    sg_ref,
-    sc_ref,
-    interp_ref,
-    out_ref,
+    *refs,
+):
+    sources, out_ref, held, rest = refs[:11], refs[11], refs[12:23], refs[23:]
+    off_ref, list_ref, cnt_ref, src_ref, p_ref, gc_ref = held[:6]
+    sb_ref, st_ref, sg_ref, sc_ref, interp_ref = held[6:]
+    (
     ext0,
     own8,
     pext,
@@ -53,32 +47,48 @@
     g_recv,
     r_send,
     r_recv,
-):
+    in_sem,
+    ) = rest
     g = lax.axis_index("grp")
     y = lax.axis_index("gy")
     z = lax.axis_index("gz")
-    rows_y, cols_z = off_ref.shape[1], off_ref.shape[2]
+    rows_y, cols_z = off_ref.shape[1], off_ref.shape[3]
+    n_near = n_gz // 2
+    half, near = z // n_near, lax.rem(z, n_near)
     guards = gc_ref.shape[3]
     slots_out = sb_ref.shape[3]
 
     def at(gg, dy, dz):
         return (gg, lax.rem(y + dy + n_gy, n_gy), lax.rem(z + dz + n_gz, n_gz))
 
-    partners = {(1, 0, o) for o in range(n_gz)}
-    partners |= {(0, o, 0) for o in range(1, n_gy)}
-    partners |= {
-        (0, a % n_gy, b % n_gz) for a in (-1, 0, 1) for b in (-1, 0, 1) if (a, b) != (0, 0)
-    }
-    partners = sorted(partners)
-
+    stage1 = sorted(
+        ((o, f) for o in range(n_gy) for f in range(2)),
+        key=lambda of: -(min(of[0] // 2, (n_gy - of[0] + 1) // 2) + 0.1 * (of[0] % 2)),
+    )
+    stage2 = sorted(range(1, n_near), key=lambda o: -min(o, n_near - o))
+
+    def at1(o, f):
+        return (1 - g, y ^ o, (half ^ f) * n_near + near)
+
+    def at2(o):
+        return (g, y, half * n_near + (near ^ o))
+
+    neighbours = [
+        (a, b) for a in (-1, 0, 1) for b in (-1, 0, 1) if (a, b) != (0, 0)
+    ]
+
+    copies = [
+        pltpu.make_async_copy(src, dst, in_sem.at[i])
+        for i, (src, dst) in enumerate(zip(sources, held))
+    ]
+    copies[10].start()
     barrier = pltpu.get_barrier_semaphore()
-    for flip, dy, dz in partners:
-        pl.semaphore_signal(
-            barrier,
-            inc=1,
-            device_id=at(1 - g if flip else g, dy, dz),
-            device_id_type=MESH,
-        )
+    people = [at1(*of) for of in stage1] + [at2(o) for o in stage2]
+    people += [at(g, *ab) for ab in neighbours]
+    for who in people:
+        pl.semaphore_signal(barrier, inc=1, device_id=who, device_id_type=MESH)
+    for i in (4, 6, 0, 7, 8, 9, 1, 2, 3, 5):
+        copies[i].start()
 
     sides = []
     for dy in (-1, 0, 1):
@@ -109,27 +119,24 @@
         pltpu.make_async_copy(part, part, sem).wait()
 
     def send_values(src, dst, sweep):
-        order = sorted(range(n_gz), key=lambda o: -min(o, n_gz - o))
-        for o in order:
+        for o, f in stage1:
             pltpu.make_async_remote_copy(
                 src_ref=src,
-                dst_ref=dst.at[o],
+                dst_ref=dst.at[2 * o + f],
                 send_sem=g_send.at[sweep],
                 recv_sem=g_recv.at[sweep],
-                device_id=at(1 - g, 0, o),
+                device_id=at1(o, f),
                 device_id_type=MESH,
             ).start()
 
     def send_buckets(sweep):
-        order = sorted(range(1, n_gy), key=lambda o: -min(o, n_gy - o))
-        for o in order:
-            to = lax.rem(y + o, n_gy)
+        for o in stage2:
             pltpu.make_async_remote_copy(
-                src_ref=buckets.at[sweep, to],
+                src_ref=buckets.at[sweep, near ^ o],
                 dst_ref=got_buckets.at[sweep, o - 1],
                 send_sem=r_send.at[sweep],
                 recv_sem=r_recv.at[sweep],
-                device_id=at(g, o, 0),
+                device_id=at2(o),
                 device_id_type=MESH,
             ).start()
 
@@ -149,15 +156,14 @@
             press = pden[pl.ds(sb_ref[0, 0, 0, s], 1), :]
             dst[pl.ds(s, 1), :] = row_sums(interp_ref[0, 0, 0, s] * press)
 
+    for i in (4, 6):
+        copies[i].wait()
     for a in range(rows_y):
-        for b in range(cols_z):
-            scaled = (off_ref[0, a, b] - 0.5) * (2.0 * KAPPA)
-            ext0[1 + a, 1 + b, pl.ds(0, 3), :] = scaled
-            ext0[1 + a, 1 + b, pl.ds(3, 1), :] = p_ref[0, a, pl.ds(b, 1), :]
-            own8[a, b, pl.ds(0, 3), :] = scaled * 0.5
         pden[pl.ds(a * cols_z, cols_z), :] = p_ref[0, a]
-
+    copies[10].wait()
     interpolate(first)
+    for i in (7, 8, 9):
+        copies[i].wait()
     codes = jnp.full((slots_out, PB), -1, jnp.int32)
     slot_row = lax.broadcasted_iota(jnp.int32, (slots_out, PB), 0)
     for s in range(slots_out):
@@ -165,9 +171,21 @@
     codes = jnp.where(slot_row < sc_ref[0, 0, 0], codes, -1)
     first[pl.ds(slots_out, slots_out), :] = codes.astype(jnp.float32)
 
-    pl.semaphore_wait(barrier, len(partners))
+    copies[0].wait()
+    for a in range(rows_y):
+        for k in range(3):
+            scaled = (off_ref[0, a, k] - 0.5) * (2.0 * KAPPA)
+            for b in range(cols_z):
+                ext0[1 + a, 1 + b, pl.ds(k, 1), :] = scaled[b : b + 1]
+                own8[a, b, pl.ds(k, 1), :] = 0.5 * scaled[b : b + 1]
+        for b in range(cols_z):
+            ext0[1 + a, 1 + b, pl.ds(3, 1), :] = p_ref[0, a, pl.ds(b, 1), :]
+
+    pl.semaphore_wait(barrier, len(people))
     send_values(first, got_first, 0)
     send_halo(ext0, 0)
+    for i in (1, 2, 3, 5):
+        copies[i].wait()
 
     for a in range(rows_y):
         lanes = lax.broadcasted_iota(jnp.int32, (cols_z, cols_z), 1)
@@ -231,7 +249,7 @@
         total = jnp.dot(sel, hi, preferred_element_type=jnp.float32)
         total += jnp.dot(sel, mid, preferred_element_type=jnp.float32)
         total += jnp.dot(sel, low, preferred_element_type=jnp.float32)
-        buckets[sweep] = total.reshape(n_gy, guards, PB)
+        buckets[sweep] = total.reshape(n_near, guards, PB)
         send_buckets(sweep)
 
     def sums(near_row, with_den):
@@ -254,19 +272,21 @@
         lax.fori_loop(0, cols_z, body, 0)
 
     lax.fori_loop(1, cols_z - 1, inner, 0)
+    rim_wait(ext0, h_recv.at[0])
+    middle = 1 + (cols_z - 2) // 2
+    lax.fori_loop(1, middle, outer, 0)
 
     whole_wait(got_first, g_recv.at[0])
-    entries = n_gz * slots_out
-    dest = n_gy * guards
+    entries = 2 * n_gy * slots_out
+    dest = n_near * guards
     code_rows = got_first[:, pl.ds(slots_out, slots_out), :].reshape(entries, PB)[:, :dest]
     lane = lax.broadcasted_iota(jnp.int32, (entries, dest), 1)
-    wanted = (lane // guards * n_gz + z) * guards + lax.rem(lane, guards)
+    wanted = (y * n_gz + half * n_near) * guards + lane
     hits = jnp.where(code_rows == wanted.astype(jnp.float32), 1.0, 0.0)
     onehot[...] = jnp.transpose(hits).astype(jnp.bfloat16)
     deliver(got_first[:, pl.ds(0, slots_out), :].reshape(entries, PB), 0)
 
-    rim_wait(ext0, h_recv.at[0])
-    lax.fori_loop(1, cols_z - 1, outer, 0)
+    lax.fori_loop(middle, cols_z - 1, outer, 0)
     lax.fori_loop(0, 2, ends, 0)
 
     sums(lambda e, k: ext0[e, k, pl.ds(3, 1), :], True)
@@ -276,8 +296,8 @@
     for sweep in range(ITERS):
         base = num[...] - src_ref[0]
         whole_wait(got_buckets.at[sweep], r_recv.at[sweep])
-        mine = buckets[sweep, y]
-        for o in range(n_gy - 1):
+        mine = buckets[sweep, near]
+        for o in range(n_near - 1):
             mine = mine + got_buckets[sweep, o]
         new = (base + coef * mine.reshape(rows_y, cols_z, PB)) * scale
         if sweep == ITERS - 1:
@@ -306,20 +326,22 @@
 
 
 def local(n_gy, n_gz, *args):
-    offsets, guard_coef, send_block = args[0], args[5], args[6]
-    rows_y, cols_z = offsets.shape[1:3]
+    args = (jnp.swapaxes(args[0], 2, 3),) + args[1:]
+    guard_coef, send_block = args[5], args[6]
+    rows_y, cols_z = args[3].shape[1:3]
     guards = guard_coef.shape[3]
     slots_out = send_block.shape[3]
+    n_near = n_gz // 2
     f32 = jnp.float32
-    vmem = pl.BlockSpec(memory_space=pltpu.VMEM)
-    smem = pl.BlockSpec(memory_space=pltpu.SMEM)
     dma = pltpu.SemaphoreType.DMA((ITERS,))
+    spaces = [pltpu.VMEM] * 6 + [pltpu.SMEM] * 4 + [pltpu.VMEM]
     return pl.pallas_call(
         functools.partial(kernel, n_gy, n_gz),
         out_shape=jax.ShapeDtypeStruct((1, rows_y, cols_z, PB), f32),
-        in_specs=[vmem] * 6 + [smem] * 4 + [vmem],
-        out_specs=vmem,
-        scratch_shapes=[
+        in_specs=[pl.BlockSpec(memory_space=pl.ANY)] * len(args),
+        out_specs=pl.BlockSpec(memory_space=pltpu.VMEM),
+        scratch_shapes=[space(a.shape, a.dtype) for space, a in zip(spaces, args)]
+        + [
             pltpu.VMEM((rows_y + 2, cols_z + 2, 4, PB), f32),
             pltpu.VMEM((rows_y, cols_z, 8, PB), f32),
             pltpu.VMEM((ITERS - 1, rows_y + 2, cols_z + 2, 1, PB), f32),
@@ -328,11 +350,11 @@
             pltpu.VMEM((SLOTS, rows_y, cols_z, PB), f32),
             pltpu.VMEM((2 * slots_out, PB), f32),
             pltpu.VMEM((ITERS - 1, slots_out, PB), f32),
-            pltpu.VMEM((n_gz, 2 * slots_out, PB), f32),
-            pltpu.VMEM((ITERS - 1, n_gz, slots_out, PB), f32),
-            pltpu.VMEM((ITERS, n_gy, guards, PB), f32),
-            pltpu.VMEM((ITERS, n_gy - 1, guards, PB), f32),
-            pltpu.VMEM((n_gy * guards, n_gz * slots_out), jnp.bfloat16),
+            pltpu.VMEM((2 * n_gy, 2 * slots_out, PB), f32),
+            pltpu.VMEM((ITERS - 1, 2 * n_gy, slots_out, PB), f32),
+            pltpu.VMEM((ITERS, n_near, guards, PB), f32),
+            pltpu.VMEM((ITERS, n_near - 1, guards, PB), f32),
+            pltpu.VMEM((n_near * guards, 2 * n_gy * slots_out), jnp.bfloat16),
             pltpu.VMEM((rows_y, cols_z, PB), f32),
             pltpu.VMEM((rows_y, cols_z, PB), f32),
             dma,
@@ -341,9 +363,10 @@
             dma,
             dma,
             dma,
+            pltpu.SemaphoreType.DMA((len(args),)),
         ],
         compiler_params=pltpu.CompilerParams(
-            collective_id=0, has_side_effects=True, vmem_limit_bytes=32 * 1024 * 1024
+            collective_id=0, has_side_effects=True, vmem_limit_bytes=60 * 1024 * 1024
         ),
     )(*args)
 

time: 45.8 us -> 42 us (0.917)
  Pallas kernels: 42.3 us -> 39.9 us
  local copies, waits for them, and re-layouts: 2.46 us -> 1.3 us
    pallas_call x1, Pallas kernels: 42.3 us -> 39.9 us  [local(): pl.pallas_call(functools.partial(kernel, n_gy, n_gz), out_shape=jax.Shape...]
    unnamed x20 -> x1, local copies, waits for them, and re-layouts: 2.46 us -> 1.3 us
where the time goes in v2:
time: 42 us; the launch traced here: 41.8 us
  Pallas kernels  39.9 us (95%)
  local copies, waits for them, and re-layouts  1.3 us (3%)
  between operations  0.66 us (2%)
    pallas_call x1, Pallas kernels, local(): pl.pallas_call(functools.partial(kernel, n_gy, n_gz), out_shape=jax.Shape...  39.9 us
    unnamed x1, local copies, waits for them, and re-layouts  1.3 us

profile of v2, /device:TPU:1, one launch (start us, length us, event | category | flops | bytes accessed | tf_op | source)
XLA Modules:
  0.0 41.8 jit_solution(8782091611845307005)
XLA Ops:
  0.7 39.9 %shard_map.109 = f32[1,2,8,128]{3,2,1,0:T(8,128)} custom-call(f32[1,2,3,8,128]{4,3,2,1,0:T(8,128)} %bitcast.1, s32[1,2,8,9]{3,2,1,0:T(8,128)} %refs_1_.1, s32[1,2,8]{2,1,0:T(2,128)} %refs_2_.1, f32[1,2,8,128]{3,2,1,0:T(8,128)} %refs_3_.1, f32[1,2,8,128]{3,2,1,0:T(8,128)} %refs_4_.1, f32[1,1,1,16,128]{4,3,2,1,0:T(8,128)} %refs_5_.1, s32[1,1,1,8]{3,2,1,0:T(1,128)} %refs_6_.1, ...), custom_call_target="tpu_custom_call" | custom-call | tf_op jit(solution)/shard_map/pallas_call | solution.py:338
  40.5 1.3 %copy.14 = f32[1,2,8,128]{3,2,1,0:T(8,128)} copy(f32[1,2,8,128]{3,2,1,0:T(8,128)} %shard_map.109) | data formatting | bytes 16384

commit v3 on v2

--- a/solution.py
+++ b/solution.py
@@ -26,28 +26,29 @@
     off_ref, list_ref, cnt_ref, src_ref, p_ref, gc_ref = held[:6]
     sb_ref, st_ref, sg_ref, sc_ref, interp_ref = held[6:]
     (
-    ext0,
-    own8,
-    pext,
-    pden,
-    wts,
-    mask,
-    first,
-    later,
-    got_first,
-    got,
-    buckets,
-    got_buckets,
-    onehot,
-    num,
-    den,
-    h_send,
-    h_recv,
-    g_send,
-    g_recv,
-    r_send,
-    r_recv,
-    in_sem,
+        ext0,
+        own8,
+        pext,
+        pden,
+        wts,
+        mask,
+        first,
+        later,
+        got_first,
+        got,
+        buckets,
+        got_buckets,
+        onehot,
+        num,
+        den,
+        h_send,
+        h_recv,
+        g_send,
+        g_recv,
+        r_send,
+        r_recv,
+        in_sem,
+        known,
     ) = rest
     g = lax.axis_index("grp")
     y = lax.axis_index("gy")
@@ -73,18 +74,19 @@
     def at2(o):
         return (g, y, half * n_near + (near ^ o))
 
-    neighbours = [
-        (a, b) for a in (-1, 0, 1) for b in (-1, 0, 1) if (a, b) != (0, 0)
-    ]
-
     copies = [
         pltpu.make_async_copy(src, dst, in_sem.at[i])
         for i, (src, dst) in enumerate(zip(sources, held))
     ]
     copies[10].start()
     barrier = pltpu.get_barrier_semaphore()
-    people = [at1(*of) for of in stage1] + [at2(o) for o in stage2]
-    people += [at(g, *ab) for ab in neighbours]
+    farthest = n_near // 2
+    beside = [at(g, 1, 0), at(g, -1, 0)]
+    beside += [
+        (g, lax.rem(y + a + n_gy, n_gy), (half ^ 1) * n_near + near) for a in (-1, 0, 1)
+    ]
+    people = [at1(*of) for of in stage1] + [at2(o) for o in stage2 if o != farthest] + beside
+    tellers = beside + [at2(1)]
     for who in people:
         pl.semaphore_signal(barrier, inc=1, device_id=who, device_id_type=MESH)
     for i in (4, 6, 0, 7, 8, 9, 1, 2, 3, 5):
@@ -101,22 +103,26 @@
             zd = {-1: cols_z + 1, 0: 1, 1: 0}[dz]
             sides.append((dy, dz, ys, zs, yd, zd))
 
-    def send_halo(buf, sweep):
-        for dy, dz, ys, zs, yd, zd in sides:
+    def send_halo(buf, sem, which):
+        for dy, dz, ys, zs, yd, zd in which:
             pltpu.make_async_remote_copy(
                 src_ref=buf.at[pl.ds(ys[0], ys[1]), pl.ds(zs[0], zs[1])],
                 dst_ref=buf.at[pl.ds(yd, ys[1]), pl.ds(zd, zs[1])],
-                send_sem=h_send.at[sweep],
-                recv_sem=h_recv.at[sweep],
+                send_sem=h_send.at[sem],
+                recv_sem=h_recv.at[sem],
                 device_id=at(g, dy, dz),
                 device_id_type=MESH,
             ).start()
 
-    rim = 2 * cols_z + 2 * rows_y + 4
-
-    def rim_wait(buf, sem):
-        part = buf.at[pl.ds(0, rim // cols_z), pl.ds(0, cols_z)]
+    rows_sides = [s for s in sides if s[1] == 0]
+    far_sides = [s for s in sides if s[1] != 0]
+
+    def rim_wait(buf, sem, blocks):
+        part = buf.at[pl.ds(0, blocks // cols_z), pl.ds(0, cols_z)]
         pltpu.make_async_copy(part, part, sem).wait()
+
+    rows_rim = 2 * cols_z
+    far_rim = 2 * rows_y + 4
 
     def send_values(src, dst, sweep):
         for o, f in stage1:
@@ -182,8 +188,10 @@
             ext0[1 + a, 1 + b, pl.ds(3, 1), :] = p_ref[0, a, pl.ds(b, 1), :]
 
     pl.semaphore_wait(barrier, len(people))
+    for who in tellers:
+        pl.semaphore_signal(known, inc=1, device_id=who, device_id_type=MESH)
     send_values(first, got_first, 0)
-    send_halo(ext0, 0)
+    send_halo(ext0, ITERS, rows_sides)
     for i in (1, 2, 3, 5):
         copies[i].wait()
 
@@ -233,12 +241,11 @@
             make_weights(a, b, [(dy, dz) for dy in dys for dz in all_dz])
         return carry
 
-    def ends(t, carry):
-        for a in range(rows_y):
-            make_weights(
-                a, t * (cols_z - 1), [(dy, dz) for dy in (-1, 0, 1) for dz in all_dz]
-            )
-        return carry
+    def ends(far):
+        for b, out in ((0, -1), (cols_z - 1, 1)):
+            for a in range(rows_y):
+                dzs = [dz for dz in all_dz if (dz == out) == far]
+                make_weights(a, b, [(dy, dz) for dy in (-1, 0, 1) for dz in dzs])
 
     def deliver(values, sweep):
         hi = values.astype(jnp.bfloat16)
@@ -252,7 +259,7 @@
         buckets[sweep] = total.reshape(n_near, guards, PB)
         send_buckets(sweep)
 
-    def sums(near_row, with_den):
+    def sums(near_row, with_den, low, high):
         def body(b, carry):
             rows = [[near_row(e, b + k) for k in range(3)] for e in range(rows_y + 2)]
             for a in range(rows_y):
@@ -269,12 +276,14 @@
                     den[a, pl.ds(b, 1), :] = row_sums(tot)
             return carry
 
-        lax.fori_loop(0, cols_z, body, 0)
+        lax.fori_loop(low, high, body, 0)
 
     lax.fori_loop(1, cols_z - 1, inner, 0)
-    rim_wait(ext0, h_recv.at[0])
-    middle = 1 + (cols_z - 2) // 2
-    lax.fori_loop(1, middle, outer, 0)
+    pl.semaphore_wait(known, len(tellers))
+    send_halo(ext0, 0, far_sides)
+    rim_wait(ext0, h_recv.at[ITERS], rows_rim)
+    lax.fori_loop(1, cols_z - 1, outer, 0)
+    ends(False)
 
     whole_wait(got_first, g_recv.at[0])
     entries = 2 * n_gy * slots_out
@@ -286,10 +295,14 @@
     onehot[...] = jnp.transpose(hits).astype(jnp.bfloat16)
     deliver(got_first[:, pl.ds(0, slots_out), :].reshape(entries, PB), 0)
 
-    lax.fori_loop(middle, cols_z - 1, outer, 0)
-    lax.fori_loop(0, 2, ends, 0)
-
-    sums(lambda e, k: ext0[e, k, pl.ds(3, 1), :], True)
+    def start_row(e, k):
+        return ext0[e, k, pl.ds(3, 1), :]
+
+    sums(start_row, True, 1, cols_z - 1)
+    rim_wait(ext0, h_recv.at[0], far_rim)
+    ends(True)
+    sums(start_row, True, 0, 1)
+    sums(start_row, True, cols_z - 1, cols_z)
     coef = gc_ref[0, 0, 0].reshape(rows_y, cols_z, PB)
     scale = 1.0 / (den[...] + coef + 1.0)
 
@@ -310,18 +323,19 @@
         for a in range(rows_y):
             for b in range(cols_z):
                 press[1 + a, 1 + b] = new[a, b : b + 1]
-        send_halo(press, sweep + 1)
-        rim_wait(press, h_recv.at[sweep + 1])
+        send_halo(press, sweep + 1, sides)
         whole_wait(got.at[sweep], g_recv.at[sweep + 1])
         deliver(got[sweep].reshape(entries, PB), sweep + 1)
-        sums(lambda e, k: press[e, k], False)
-
-    rim_wait(ext0, h_send.at[0])
+        rim_wait(press, h_recv.at[sweep + 1], rows_rim + far_rim)
+        sums(lambda e, k: press[e, k], False, 0, cols_z)
+
+    rim_wait(ext0, h_send.at[ITERS], rows_rim)
+    rim_wait(ext0, h_send.at[0], far_rim)
     whole_wait(got_first, g_send.at[0])
     for sweep in range(ITERS):
         whole_wait(got_buckets.at[sweep], r_send.at[sweep])
         if sweep:
-            rim_wait(pext.at[sweep - 1], h_send.at[sweep])
+            rim_wait(pext.at[sweep - 1], h_send.at[sweep], rows_rim + far_rim)
             whole_wait(got.at[sweep - 1], g_send.at[sweep])
 
 
@@ -334,6 +348,7 @@
     n_near = n_gz // 2
     f32 = jnp.float32
     dma = pltpu.SemaphoreType.DMA((ITERS,))
+    halo_dma = pltpu.SemaphoreType.DMA((ITERS + 1,))
     spaces = [pltpu.VMEM] * 6 + [pltpu.SMEM] * 4 + [pltpu.VMEM]
     return pl.pallas_call(
         functools.partial(kernel, n_gy, n_gz),
@@ -357,13 +372,14 @@
             pltpu.VMEM((n_near * guards, 2 * n_gy * slots_out), jnp.bfloat16),
             pltpu.VMEM((rows_y, cols_z, PB), f32),
             pltpu.VMEM((rows_y, cols_z, PB), f32),
-            dma,
-            dma,
+            halo_dma,
+            halo_dma,
             dma,
             dma,
             dma,
             dma,
             pltpu.SemaphoreType.DMA((len(args),)),
+            pltpu.SemaphoreType.REGULAR,
         ],
         compiler_params=pltpu.CompilerParams(
             collective_id=0, has_side_effects=True, vmem_limit_bytes=60 * 1024 * 1024

time: 42 us -> 43.3 us (1.031)
  Pallas kernels: 39.9 us -> 41.2 us
    pallas_call x1, Pallas kernels: 39.9 us -> 41.2 us  [local(): pl.pallas_call(functools.partial(kernel, n_gy, n_gz), out_shape=jax.Shape...]
where the time goes in v3:
time: 43.3 us; the launch traced here: 43.2 us
  Pallas kernels  41.2 us (95%)
  local copies, waits for them, and re-layouts  1.3 us (3%)
  between operations  0.66 us (2%)
    pallas_call x1, Pallas kernels, local(): pl.pallas_call(functools.partial(kernel, n_gy, n_gz), out_shape=jax.Shape...  41.2 us
    unnamed x1, local copies, waits for them, and re-layouts  1.3 us

profile of v3, /device:TPU:1, one launch (start us, length us, event | category | flops | bytes accessed | tf_op | source)
XLA Modules:
  0.0 43.2 jit_solution(14274042061423508057)
XLA Ops:
  0.7 41.2 %shard_map.109 = f32[1,2,8,128]{3,2,1,0:T(8,128)} custom-call(f32[1,2,3,8,128]{4,3,2,1,0:T(8,128)} %bitcast.1, s32[1,2,8,9]{3,2,1,0:T(8,128)} %refs_1_.1, s32[1,2,8]{2,1,0:T(2,128)} %refs_2_.1, f32[1,2,8,128]{3,2,1,0:T(8,128)} %refs_3_.1, f32[1,2,8,128]{3,2,1,0:T(8,128)} %refs_4_.1, f32[1,1,1,16,128]{4,3,2,1,0:T(8,128)} %refs_5_.1, s32[1,1,1,8]{3,2,1,0:T(1,128)} %refs_6_.1, ...), custom_call_target="tpu_custom_call" | custom-call | tf_op jit(solution)/shard_map/pallas_call | solution.py:353
  41.9 1.3 %copy.14 = f32[1,2,8,128]{3,2,1,0:T(8,128)} copy(f32[1,2,8,128]{3,2,1,0:T(8,128)} %shard_map.109) | data formatting | bytes 16384

commit v4 on v3

--- a/solution.py
+++ b/solution.py
@@ -281,10 +281,6 @@
     lax.fori_loop(1, cols_z - 1, inner, 0)
     pl.semaphore_wait(known, len(tellers))
     send_halo(ext0, 0, far_sides)
-    rim_wait(ext0, h_recv.at[ITERS], rows_rim)
-    lax.fori_loop(1, cols_z - 1, outer, 0)
-    ends(False)
-
     whole_wait(got_first, g_recv.at[0])
     entries = 2 * n_gy * slots_out
     dest = n_near * guards
@@ -294,6 +290,10 @@
     hits = jnp.where(code_rows == wanted.astype(jnp.float32), 1.0, 0.0)
     onehot[...] = jnp.transpose(hits).astype(jnp.bfloat16)
     deliver(got_first[:, pl.ds(0, slots_out), :].reshape(entries, PB), 0)
+
+    rim_wait(ext0, h_recv.at[ITERS], rows_rim)
+    lax.fori_loop(1, cols_z - 1, outer, 0)
+    ends(False)
 
     def start_row(e, k):
         return ext0[e, k, pl.ds(3, 1), :]
@@ -352,7 +352,7 @@
     spaces = [pltpu.VMEM] * 6 + [pltpu.SMEM] * 4 + [pltpu.VMEM]
     return pl.pallas_call(
         functools.partial(kernel, n_gy, n_gz),
-        out_shape=jax.ShapeDtypeStruct((1, rows_y, cols_z, PB), f32),
+        out_shape=pltpu.VMEM((1, rows_y, cols_z, PB), f32),
         in_specs=[pl.BlockSpec(memory_space=pl.ANY)] * len(args),
         out_specs=pl.BlockSpec(memory_space=pltpu.VMEM),
         scratch_shapes=[space(a.shape, a.dtype) for space, a in zip(spaces, args)]

time: 43.3 us -> 40.7 us (0.940)
  Pallas kernels: 41.2 us -> 39.4 us
  local copies, waits for them, and re-layouts: 1.3 us -> 0.6 us
    pallas_call x1, Pallas kernels: 41.2 us -> 39.4 us  [local(): pl.pallas_call(functools.partial(kernel, n_gy, n_gz), out_shape=pltpu.VME...]
    unnamed x1, local copies, waits for them, and re-layouts: 1.3 us -> 0.6 us
where the time goes in v4:
time: 40.7 us; the launch traced here: 40.6 us
  Pallas kernels  39.4 us (97%)
  between operations  0.66 us (2%)
  local copies, waits for them, and re-layouts  0.6 us (1%)
    pallas_call x1, Pallas kernels, local(): pl.pallas_call(functools.partial(kernel, n_gy, n_gz), out_shape=pltpu.VME...  39.4 us

profile of v4, /device:TPU:1, one launch (start us, length us, event | category | flops | bytes accessed | tf_op | source)
XLA Modules:
  0.0 40.6 jit_solution(17202764919622194405)
XLA Ops:
  0.7 39.4 %shard_map.109 = f32[1,2,8,128]{3,2,1,0:T(8,128)S(1)} custom-call(f32[1,2,3,8,128]{4,3,2,1,0:T(8,128)} %bitcast.1, s32[1,2,8,9]{3,2,1,0:T(8,128)} %refs_1_.1, s32[1,2,8]{2,1,0:T(2,128)} %refs_2_.1, f32[1,2,8,128]{3,2,1,0:T(8,128)} %refs_3_.1, f32[1,2,8,128]{3,2,1,0:T(8,128)} %refs_4_.1, f32[1,1,1,16,128]{4,3,2,1,0:T(8,128)} %refs_5_.1, ...), custom_call_target="tpu_custom_call" | custom-call | tf_op jit(solution)/shard_map/pallas_call | solution.py:353
  40.0 0.6 %copy.13 = f32[1,2,8,128]{3,2,1,0:T(8,128)} copy(f32[1,2,8,128]{3,2,1,0:T(8,128)S(1)} %shard_map.109) | data formatting | bytes 16384

commit v5 on v4

--- a/solution.py
+++ b/solution.py
@@ -78,7 +78,8 @@
         pltpu.make_async_copy(src, dst, in_sem.at[i])
         for i, (src, dst) in enumerate(zip(sources, held))
     ]
-    copies[10].start()
+    for i in (4, 6, 10):
+        copies[i].start()
     barrier = pltpu.get_barrier_semaphore()
     farthest = n_near // 2
     beside = [at(g, 1, 0), at(g, -1, 0)]
@@ -89,7 +90,7 @@
     tellers = beside + [at2(1)]
     for who in people:
         pl.semaphore_signal(barrier, inc=1, device_id=who, device_id_type=MESH)
-    for i in (4, 6, 0, 7, 8, 9, 1, 2, 3, 5):
+    for i in (7, 8, 9, 0, 1, 2, 3, 5):
         copies[i].start()
 
     sides = []
@@ -177,6 +178,11 @@
     codes = jnp.where(slot_row < sc_ref[0, 0, 0], codes, -1)
     first[pl.ds(slots_out, slots_out), :] = codes.astype(jnp.float32)
 
+    pl.semaphore_wait(barrier, len(people))
+    for who in tellers:
+        pl.semaphore_signal(known, inc=1, device_id=who, device_id_type=MESH)
+    send_values(first, got_first, 0)
+
     copies[0].wait()
     for a in range(rows_y):
         for k in range(3):
@@ -186,11 +192,6 @@
                 own8[a, b, pl.ds(k, 1), :] = 0.5 * scaled[b : b + 1]
         for b in range(cols_z):
             ext0[1 + a, 1 + b, pl.ds(3, 1), :] = p_ref[0, a, pl.ds(b, 1), :]
-
-    pl.semaphore_wait(barrier, len(people))
-    for who in tellers:
-        pl.semaphore_signal(known, inc=1, device_id=who, device_id_type=MESH)
-    send_values(first, got_first, 0)
     send_halo(ext0, ITERS, rows_sides)
     for i in (1, 2, 3, 5):
         copies[i].wait()
@@ -281,6 +282,9 @@
     lax.fori_loop(1, cols_z - 1, inner, 0)
     pl.semaphore_wait(known, len(tellers))
     send_halo(ext0, 0, far_sides)
+    rim_wait(ext0, h_recv.at[ITERS], rows_rim)
+    middle = cols_z // 2
+    lax.fori_loop(1, middle, outer, 0)
     whole_wait(got_first, g_recv.at[0])
     entries = 2 * n_gy * slots_out
     dest = n_near * guards
@@ -291,8 +295,7 @@
     onehot[...] = jnp.transpose(hits).astype(jnp.bfloat16)
     deliver(got_first[:, pl.ds(0, slots_out), :].reshape(entries, PB), 0)
 
-    rim_wait(ext0, h_recv.at[ITERS], rows_rim)
-    lax.fori_loop(1, cols_z - 1, outer, 0)
+    lax.fori_loop(middle, cols_z - 1, outer, 0)
     ends(False)
 
     def start_row(e, k):

time: 40.7 us -> 40.2 us (0.988)
  Pallas kernels: 39.4 us -> 38.8 us
    pallas_call x1, Pallas kernels: 39.4 us -> 38.8 us  [local(): pl.pallas_call(functools.partial(kernel, n_gy, n_gz), out_shape=pltpu.VME...]
where the time goes in v5:
time: 40.2 us; the launch traced here: 40.1 us
  Pallas kernels  38.8 us (97%)
  between operations  0.66 us (2%)
  local copies, waits for them, and re-layouts  0.6 us (1%)
    pallas_call x1, Pallas kernels, local(): pl.pallas_call(functools.partial(kernel, n_gy, n_gz), out_shape=pltpu.VME...  38.8 us

profile of v5, /device:TPU:1, one launch (start us, length us, event | category | flops | bytes accessed | tf_op | source)
XLA Modules:
  0.0 40.1 jit_solution(2373800423086364406)
XLA Ops:
  0.7 38.8 %shard_map.109 = f32[1,2,8,128]{3,2,1,0:T(8,128)S(1)} custom-call(f32[1,2,3,8,128]{4,3,2,1,0:T(8,128)} %bitcast.1, s32[1,2,8,9]{3,2,1,0:T(8,128)} %refs_1_.1, s32[1,2,8]{2,1,0:T(2,128)} %refs_2_.1, f32[1,2,8,128]{3,2,1,0:T(8,128)} %refs_3_.1, f32[1,2,8,128]{3,2,1,0:T(8,128)} %refs_4_.1, f32[1,1,1,16,128]{4,3,2,1,0:T(8,128)} %refs_5_.1, ...), custom_call_target="tpu_custom_call" | custom-call | tf_op jit(solution)/shard_map/pallas_call | solution.py:356
  39.5 0.6 %copy.13 = f32[1,2,8,128]{3,2,1,0:T(8,128)} copy(f32[1,2,8,128]{3,2,1,0:T(8,128)S(1)} %shard_map.109) | data formatting | bytes 16384

commit v6 on v5

--- a/solution.py
+++ b/solution.py
@@ -62,11 +62,10 @@
     def at(gg, dy, dz):
         return (gg, lax.rem(y + dy + n_gy, n_gy), lax.rem(z + dz + n_gz, n_gz))
 
-    stage1 = sorted(
-        ((o, f) for o in range(n_gy) for f in range(2)),
-        key=lambda of: -(min(of[0] // 2, (n_gy - of[0] + 1) // 2) + 0.1 * (of[0] % 2)),
-    )
-    stage2 = sorted(range(1, n_near), key=lambda o: -min(o, n_near - o))
+    across = [o for o in (4, 5, 6, 7, 2, 3, 1, 0) if o < n_gy]
+    stage1 = [(o, 1) for o in across[:6]] + [(o, 0) for o in across[:4]]
+    stage1 += [(o, 1) for o in across[6:]] + [(o, 0) for o in across[4:]]
+    stage2 = [o for o in (4, 5, 7, 6, 3, 2, 1) if o < n_near]
 
     def at1(o, f):
         return (1 - g, y ^ o, (half ^ f) * n_near + near)
@@ -250,13 +249,9 @@
 
     def deliver(values, sweep):
         hi = values.astype(jnp.bfloat16)
-        rest = values - hi.astype(jnp.float32)
-        mid = rest.astype(jnp.bfloat16)
-        low = (rest - mid.astype(jnp.float32)).astype(jnp.bfloat16)
-        sel = onehot[...]
-        total = jnp.dot(sel, hi, preferred_element_type=jnp.float32)
-        total += jnp.dot(sel, mid, preferred_element_type=jnp.float32)
-        total += jnp.dot(sel, low, preferred_element_type=jnp.float32)
+        low = (values - hi.astype(jnp.float32)).astype(jnp.bfloat16)
+        both = jnp.concatenate([hi, low], axis=0)
+        total = jnp.dot(onehot[...], both, preferred_element_type=jnp.float32)
         buckets[sweep] = total.reshape(n_near, guards, PB)
         send_buckets(sweep)
 
@@ -292,7 +287,8 @@
     lane = lax.broadcasted_iota(jnp.int32, (entries, dest), 1)
     wanted = (y * n_gz + half * n_near) * guards + lane
     hits = jnp.where(code_rows == wanted.astype(jnp.float32), 1.0, 0.0)
-    onehot[...] = jnp.transpose(hits).astype(jnp.bfloat16)
+    chosen = jnp.transpose(hits).astype(jnp.bfloat16)
+    onehot[...] = jnp.concatenate([chosen, chosen], axis=1)
     deliver(got_first[:, pl.ds(0, slots_out), :].reshape(entries, PB), 0)
 
     lax.fori_loop(middle, cols_z - 1, outer, 0)
@@ -372,7 +368,7 @@
             pltpu.VMEM((ITERS - 1, 2 * n_gy, slots_out, PB), f32),
             pltpu.VMEM((ITERS, n_near, guards, PB), f32),
             pltpu.VMEM((ITERS, n_near - 1, guards, PB), f32),
-            pltpu.VMEM((n_near * guards, 2 * n_gy * slots_out), jnp.bfloat16),
+            pltpu.VMEM((n_near * guards, 4 * n_gy * slots_out), jnp.bfloat16),
             pltpu.VMEM((rows_y, cols_z, PB), f32),
             pltpu.VMEM((rows_y, cols_z, PB), f32),
             halo_dma,

time: 40.2 us -> 40.1 us (level)
  no operation moved by 1% of the time
where the time goes in v6:
time: 40.1 us; the launch traced here: 40 us
  Pallas kernels  38.7 us (97%)
  between operations  0.66 us (2%)
  local copies, waits for them, and re-layouts  0.6 us (1%)
    pallas_call x1, Pallas kernels, local(): pl.pallas_call(functools.partial(kernel, n_gy, n_gz), out_shape=pltpu.VME...  38.7 us

profile of v6, /device:TPU:1, one launch (start us, length us, event | category | flops | bytes accessed | tf_op | source)
XLA Modules:
  0.0 40.0 jit_solution(7560540301846366857)
XLA Ops:
  0.7 38.7 %shard_map.109 = f32[1,2,8,128]{3,2,1,0:T(8,128)S(1)} custom-call(f32[1,2,3,8,128]{4,3,2,1,0:T(8,128)} %bitcast.1, s32[1,2,8,9]{3,2,1,0:T(8,128)} %refs_1_.1, s32[1,2,8]{2,1,0:T(2,128)} %refs_2_.1, f32[1,2,8,128]{3,2,1,0:T(8,128)} %refs_3_.1, f32[1,2,8,128]{3,2,1,0:T(8,128)} %refs_4_.1, f32[1,1,1,16,128]{4,3,2,1,0:T(8,128)} %refs_5_.1, ...), custom_call_target="tpu_custom_call" | custom-call | tf_op jit(solution)/shard_map/pallas_call | solution.py:352
  39.4 0.6 %copy.13 = f32[1,2,8,128]{3,2,1,0:T(8,128)} copy(f32[1,2,8,128]{3,2,1,0:T(8,128)S(1)} %shard_map.109) | data formatting | bytes 16384

commit v7 on v6

--- a/solution.py
+++ b/solution.py
@@ -305,16 +305,16 @@
     coef = gc_ref[0, 0, 0].reshape(rows_y, cols_z, PB)
     scale = 1.0 / (den[...] + coef + 1.0)
 
-    for sweep in range(ITERS):
+    def updated(sweep):
         base = num[...] - src_ref[0]
         whole_wait(got_buckets.at[sweep], r_recv.at[sweep])
         mine = buckets[sweep, near]
         for o in range(n_near - 1):
             mine = mine + got_buckets[sweep, o]
-        new = (base + coef * mine.reshape(rows_y, cols_z, PB)) * scale
-        if sweep == ITERS - 1:
-            out_ref[0] = new
-            break
+        return (base + coef * mine.reshape(rows_y, cols_z, PB)) * scale
+
+    def one_sweep(sweep, carry):
+        new = updated(sweep)
         pden[...] = new.reshape(rows_y * cols_z, PB)
         interpolate(later.at[sweep])
         send_values(later.at[sweep], got.at[sweep], sweep + 1)
@@ -327,6 +327,10 @@
         deliver(got[sweep].reshape(entries, PB), sweep + 1)
         rim_wait(press, h_recv.at[sweep + 1], rows_rim + far_rim)
         sums(lambda e, k: press[e, k], False, 0, cols_z)
+        return carry
+
+    lax.fori_loop(0, ITERS - 1, one_sweep, 0)
+    out_ref[0] = updated(ITERS - 1)
 
     rim_wait(ext0, h_send.at[ITERS], rows_rim)
     rim_wait(ext0, h_send.at[0], far_rim)

time: 40.1 us -> 40 us (level)
  no operation moved by 1% of the time
where the time goes in v7:
time: 40 us; the launch traced here: 39.9 us
  Pallas kernels  38.6 us (96%)
  between operations  0.66 us (2%)
  local copies, waits for them, and re-layouts  0.6 us (2%)
    pallas_call x1, Pallas kernels, local(): pl.pallas_call(functools.partial(kernel, n_gy, n_gz), out_shape=pltpu.VME...  38.6 us

profile of v7, /device:TPU:1, one launch (start us, length us, event | category | flops | bytes accessed | tf_op | source)
XLA Modules:
  0.0 39.9 jit_solution(17831003246235684)
XLA Ops:
  0.7 38.6 %shard_map.109 = f32[1,2,8,128]{3,2,1,0:T(8,128)S(1)} custom-call(f32[1,2,3,8,128]{4,3,2,1,0:T(8,128)} %bitcast.1, s32[1,2,8,9]{3,2,1,0:T(8,128)} %refs_1_.1, s32[1,2,8]{2,1,0:T(2,128)} %refs_2_.1, f32[1,2,8,128]{3,2,1,0:T(8,128)} %refs_3_.1, f32[1,2,8,128]{3,2,1,0:T(8,128)} %refs_4_.1, f32[1,1,1,16,128]{4,3,2,1,0:T(8,128)} %refs_5_.1, ...), custom_call_target="tpu_custom_call" | custom-call | tf_op jit(solution)/shard_map/pallas_call | solution.py:356
  39.3 0.6 %copy.13 = f32[1,2,8,128]{3,2,1,0:T(8,128)} copy(f32[1,2,8,128]{3,2,1,0:T(8,128)S(1)} %shard_map.109) | data formatting | bytes 16384

commit v8 on v6

--- a/solution.py
+++ b/solution.py
@@ -49,6 +49,7 @@
         r_recv,
         in_sem,
         known,
+        far_bucket,
     ) = rest
     g = lax.axis_index("grp")
     y = lax.axis_index("gy")
@@ -135,16 +136,15 @@
                 device_id_type=MESH,
             ).start()
 
-    def send_buckets(sweep):
-        for o in stage2:
-            pltpu.make_async_remote_copy(
-                src_ref=buckets.at[sweep, near ^ o],
-                dst_ref=got_buckets.at[sweep, o - 1],
-                send_sem=r_send.at[sweep],
-                recv_sem=r_recv.at[sweep],
-                device_id=at2(o),
-                device_id_type=MESH,
-            ).start()
+    def send_bucket(src, o, sweep):
+        pltpu.make_async_remote_copy(
+            src_ref=src,
+            dst_ref=got_buckets.at[sweep, o - 1],
+            send_sem=r_send.at[sweep],
+            recv_sem=r_recv.at[sweep],
+            device_id=at2(o),
+            device_id_type=MESH,
+        ).start()
 
     def whole_wait(ref, sem):
         pltpu.make_async_copy(ref, ref, sem).wait()
@@ -251,9 +251,14 @@
         hi = values.astype(jnp.bfloat16)
         low = (values - hi.astype(jnp.float32)).astype(jnp.bfloat16)
         both = jnp.concatenate([hi, low], axis=0)
+        o = stage2[0]
+        rows = pl.ds(pl.multiple_of((near ^ o) * guards, guards), guards)
+        far_bucket[sweep] = jnp.dot(onehot[rows, :], both, preferred_element_type=jnp.float32)
+        send_bucket(far_bucket.at[sweep], o, sweep)
         total = jnp.dot(onehot[...], both, preferred_element_type=jnp.float32)
         buckets[sweep] = total.reshape(n_near, guards, PB)
-        send_buckets(sweep)
+        for o in stage2[1:]:
+            send_bucket(buckets.at[sweep, near ^ o], o, sweep)
 
     def sums(near_row, with_den, low, high):
         def body(b, carry):
@@ -379,6 +384,7 @@
             dma,
             pltpu.SemaphoreType.DMA((len(args),)),
             pltpu.SemaphoreType.REGULAR,
+            pltpu.VMEM((ITERS, guards, PB), f32),
         ],
         compiler_params=pltpu.CompilerParams(
             collective_id=0, has_side_effects=True, vmem_limit_bytes=60 * 1024 * 1024

time: 40.1 us -> 40 us (level)
  no operation moved by 1% of the time
where the time goes in v8:
time: 40 us; the launch traced here: 39.9 us
  Pallas kernels  38.6 us (96%)
  between operations  0.66 us (2%)
  local copies, waits for them, and re-layouts  0.6 us (2%)
    pallas_call x1, Pallas kernels, local(): pl.pallas_call(functools.partial(kernel, n_gy, n_gz), out_shape=pltpu.VME...  38.6 us

profile of v8, /device:TPU:1, one launch (start us, length us, event | category | flops | bytes accessed | tf_op | source)
XLA Modules:
  0.0 39.9 jit_solution(1634382843421624243)
XLA Ops:
  0.7 38.6 %shard_map.109 = f32[1,2,8,128]{3,2,1,0:T(8,128)S(1)} custom-call(f32[1,2,3,8,128]{4,3,2,1,0:T(8,128)} %bitcast.1, s32[1,2,8,9]{3,2,1,0:T(8,128)} %refs_1_.1, s32[1,2,8]{2,1,0:T(2,128)} %refs_2_.1, f32[1,2,8,128]{3,2,1,0:T(8,128)} %refs_3_.1, f32[1,2,8,128]{3,2,1,0:T(8,128)} %refs_4_.1, f32[1,1,1,16,128]{4,3,2,1,0:T(8,128)} %refs_5_.1, ...), custom_call_target="tpu_custom_call" | custom-call | tf_op jit(solution)/shard_map/pallas_call | solution.py:357
  39.3 0.6 %copy.13 = f32[1,2,8,128]{3,2,1,0:T(8,128)} copy(f32[1,2,8,128]{3,2,1,0:T(8,128)S(1)} %shard_map.109) | data formatting | bytes 16384

commit v9 on v6

--- a/solution.py
+++ b/solution.py
@@ -304,14 +304,16 @@
     sums(start_row, True, cols_z - 1, cols_z)
     coef = gc_ref[0, 0, 0].reshape(rows_y, cols_z, PB)
     scale = 1.0 / (den[...] + coef + 1.0)
+    weight = coef * scale
 
     for sweep in range(ITERS):
-        base = num[...] - src_ref[0]
+        base = (num[...] - src_ref[0]) * scale
+        own = buckets[sweep, near]
         whole_wait(got_buckets.at[sweep], r_recv.at[sweep])
-        mine = buckets[sweep, near]
+        mine = own
         for o in range(n_near - 1):
             mine = mine + got_buckets[sweep, o]
-        new = (base + coef * mine.reshape(rows_y, cols_z, PB)) * scale
+        new = base + weight * mine.reshape(rows_y, cols_z, PB)
         if sweep == ITERS - 1:
             out_ref[0] = new
             break

time: 40.1 us -> 40.1 us (level)
  no operation moved by 1% of the time
where the time goes in v9:
time: 40.1 us; the launch traced here: 40 us
  Pallas kernels  38.7 us (97%)
  between operations  0.66 us (2%)
  local copies, waits for them, and re-layouts  0.6 us (1%)
    pallas_call x1, Pallas kernels, local(): pl.pallas_call(functools.partial(kernel, n_gy, n_gz), out_shape=pltpu.VME...  38.7 us

profile of v9, /device:TPU:1, one launch (start us, length us, event | category | flops | bytes accessed | tf_op | source)
XLA Modules:
  0.0 40.0 jit_solution(10102538147968205767)
XLA Ops:
  0.7 38.7 %shard_map.109 = f32[1,2,8,128]{3,2,1,0:T(8,128)S(1)} custom-call(f32[1,2,3,8,128]{4,3,2,1,0:T(8,128)} %bitcast.1, s32[1,2,8,9]{3,2,1,0:T(8,128)} %refs_1_.1, s32[1,2,8]{2,1,0:T(2,128)} %refs_2_.1, f32[1,2,8,128]{3,2,1,0:T(8,128)} %refs_3_.1, f32[1,2,8,128]{3,2,1,0:T(8,128)} %refs_4_.1, f32[1,1,1,16,128]{4,3,2,1,0:T(8,128)} %refs_5_.1, ...), custom_call_target="tpu_custom_call" | custom-call | tf_op jit(solution)/shard_map/pallas_call | solution.py:354
  39.4 0.6 %copy.13 = f32[1,2,8,128]{3,2,1,0:T(8,128)} copy(f32[1,2,8,128]{3,2,1,0:T(8,128)S(1)} %shard_map.109) | data formatting | bytes 16384
